TPU v7x, 512 devices: a whole 4x4x16 slice. The times are simulated.
512 devices in a mesh: tm: 4 (over x), height: 8 (over z_lo, core), chan: 16 (over z_hi, y).
Axes of the slice: x: 4, y: 4, z: 16 (z_hi: 4, z_lo: 4; z = z_hi * 4 + z_lo), core: 2. Of those that a mesh axis runs over, the one named last changes fastest.
Arguments:
- features: bfloat16 [384, 8, 32, 160], P('chan', 'tm', 'height'), may hold values from -400 to 400, as said below
- cotangent: bfloat16 [384, 8, 32, 160], P('chan', 'tm', 'height'), may hold values from -6 to 6
- conv_weight: bfloat16 [384, 27, 384], P('chan'), may hold values from -0.0625 to 0.0625
- norm_gain: float32 [384], replicated, may hold values from 0.5 to 1.5
- norm_bias: float32 [384], replicated, may hold values from -3 to 3
Outputs:
- input_grad: bfloat16 [384, 8, 32, 160], P('chan', 'tm', 'height')
- weight_grad: float32 [384, 27, 384], P('chan')
Inputs may be any that keep to these rules, and one draw needn't show every extreme that they name: `features`: bounded activations.
All inputs are finite; a program needn't handle non-finite values.
Results may differ from a plain program's by a relative error of at most 0.003.
Values may be sent and summed in bfloat16 or wider, within the bound.
A program may use at most 64 MiB of HBM per device.

v0:
```python
import math
import jax
import jax.numpy as jnp
from jax import lax
from jax.sharding import PartitionSpec as P


def from_behind(block, axis, distance):
    devices = range(lax.axis_size(axis))
    route = [(i - distance, i) for i in devices if i - distance in devices]
    return lax.ppermute(block, axis, route)


def with_halo(array, sides, width):
    for axis, dim in sides:
        size, length = (lax.axis_size(axis), array.shape[dim])
        up = [(i, (i + 1) % size) for i in range(size - 1)]
        down = [(j, i) for i, j in up]
        last = lax.slice_in_dim(array, length - width, length, axis=dim)
        first = lax.slice_in_dim(array, 0, width, axis=dim)
        before = lax.ppermute(last, axis, up)
        after = lax.ppermute(first, axis, down)
        array = jnp.concatenate([before, array, after], axis=dim)
    return array


def on_device(features, cotangent, conv_weight, norm_gain, norm_bias):
    chans, frames, rows, cols = features.shape
    whole_x = lax.all_gather(features, "chan", axis=0, tiled=True)
    total = whole_x.shape[0]
    flat_x = whole_x.reshape(total, -1).astype(jnp.float32)
    inv_rms = lax.rsqrt(jnp.mean(flat_x * flat_x, axis=0, keepdims=True) + 1e-06)
    normed = flat_x * inv_rms * norm_gain[:, None] + norm_bias[:, None]
    active = jax.nn.silu(normed).astype(jnp.bfloat16)
    ahead = from_behind(cotangent, "tm", -1)
    longer = jnp.concatenate([cotangent, ahead], axis=1)
    bordered = with_halo(longer, (("height", 2),), 1)
    padded = jnp.pad(bordered, ((0, 0), (0, 0), (0, 0), (1, 1)))
    taps = []
    for kt in range(3):
        for kh in range(3):
            for kw in range(3):
                taps.append(
                    padded[
                        :, 2 - kt : 2 - kt + frames, 2 - kh : 2 - kh + rows, 2 - kw : 2 - kw + cols
                    ]
                )
    stacked = jnp.stack(taps, axis=1).reshape(chans * 27, -1)
    local_sums = lax.dot_general(
        stacked, active, (((1,), (1,)), ((), ())), preferred_element_type=jnp.float32
    )
    positions = frames * lax.axis_size("tm") * rows * lax.axis_size("height") * cols
    summed = lax.psum(local_sums, ("tm", "height"))
    weight_grad = (summed / math.sqrt(positions)).reshape(chans, 27, total)
    sig = jax.nn.sigmoid(normed)
    slope = sig * (1.0 + normed * (1.0 - sig))
    offset = lax.axis_index("chan") * chans
    weight_flat = conv_weight.reshape(chans * 27, total)
    partial_value = lax.dot_general(
        weight_flat, stacked, (((0,), (0,)), ((), ())), preferred_element_type=jnp.float32
    )
    act_grad = lax.psum(partial_value, "chan")
    upstream = act_grad * slope * norm_gain[:, None]
    dots = jnp.sum(upstream * flat_x, axis=0, keepdims=True)
    back = inv_rms * upstream - flat_x * inv_rms**3 * dots / total
    own_back = lax.dynamic_slice_in_dim(back, offset, chans, 0)
    result = cotangent.reshape(chans, -1).astype(jnp.float32) + own_back
    return (result.astype(jnp.bfloat16).reshape(features.shape), weight_grad)


def solution(mesh):
    return jax.shard_map(
        on_device,
        mesh=mesh,
        in_specs=(
            P("chan", "tm", "height", None),
            P("chan", "tm", "height", None),
            P("chan", None, None),
            P(),
            P(),
        ),
        out_specs=(P("chan", "tm", "height", None), P("chan", None, None)),
        check_vma=False,
    )
```

profile of v0, /device:TPU:6, one launch (start us, length us, event | category | flops | bytes accessed | tf_op | source)
XLA Modules:
  0.0 687.3 jit_solution(8743268547803639951)
XLA Ops:
  7.2 2.7 collective-permute-start
  10.0 96.6 %all_gather.3 = bf16[384,2,4,160]{3,2,1,0:T(4,128)(2,1)S(1)} all-gather(bf16[24,2,4,160]{3,2,1,0:T(4,128)(2,1)} %param.5), channel_id=1, replica_groups=mesh['tm'=4,'height'=8,'chan'=16] {'chan'}, dimensions={0}, use_global_device_ids=true | all-gather | bytes 1044480 | tf_op jit(solution)/shard_map/all_gather | solution.py:29
  106.5 1.4 copy.18
  108.0 0.4 multiply_reduce_fusion.1
  108.5 0.1 fusion.38
  108.6 1.9 collective-permute-start.1
  110.5 1.3 collective-permute-start.2
  111.8 1.7 multiply_convert_fusion
  113.5 0.2 collective-permute-done.2
  113.7 0.8 fusion.10
  114.5 0.1 fusion.37
  114.6 0.2 fusion.36
  114.8 0.1 fusion.35
  114.9 0.2 fusion.34
  115.1 0.1 fusion.33
  115.2 0.1 fusion.32
  115.3 0.1 fusion.31
  115.5 0.2 fusion.29
  115.7 0.2 fusion.28
  115.9 0.2 fusion.26
  116.1 0.1 fusion.24
  116.2 0.1 fusion.23
  116.3 0.1 fusion.22
  116.5 0.2 fusion.20
  116.7 0.2 fusion.19
  116.9 0.1 fusion.17
  116.9 0.2 fusion.16
  117.1 0.1 fusion.15
  117.2 0.1 fusion.14
  117.4 0.1 fusion.13
  117.6 2.4 copy.19
  120.0 5.5 reshape.64
  125.5 3.2 fusion.39
  128.7 0.2 all-reduce.4.cloned.1.call-start
  128.9 1.1 copy.20
  130.0 1.0 reshape.65
  131.0 3.6 convolution_bitcast_fusion
  134.6 0.1 rsqrt.16
  134.6 1.0 copy.17
  135.7 1.5 bitcast_convert_fusion
  137.2 261.6 %all-reduce.6.cloned.1.call-done = f32[648,384]{1,0:T(8,128)} async-done(((f32[648,384]{1,0:T(8,128)}), f32[648,384]{1,0:T(8,128)}) %all-reduce.6.cloned.1.call-update) | async-done | bytes 995344 | tf_op jit(solution)/shard_map/psum | solution.py:53
  398.7 1.3 broadcast_multiply_fusion
  400.0 0.1 reshape.67
  400.2 1.5 copy.22
  401.7 272.7 %all-reduce.4.cloned.1.call-done = f32[384,1280]{0,1:T(8,128)} async-done(((f32[384,1280]{0,1:T(8,128)}), f32[384,1280]{0,1:T(8,128)}) %all-reduce.4.cloned.1.call-update) | async-done | bytes 1966096 | tf_op jit(solution)/shard_map/psum | solution.py:62
  674.4 3.0 multiply_reduce_fusion
  677.3 2.2 fusion.3
  679.6 0.8 copy.21
  (24 shorter events, 0.5 us)
Async XLA Ops:
  7.2 101.2 %copy-start.1 = (bf16[24,2,4,160]{3,2,1,0:T(4,128)(2,1)S(1)}, bf16[24,2,4,160]{3,2,1,0:T(4,128)(2,1)}, u32[]{:S(2)}) copy-start(bf16[24,2,4,160]{3,2,1,0:T(4,128)(2,1)} %param.6) | copy-start | bytes 184324
  7.2 104.6 %copy-start.3 = (f32[384]{0:T(512)S(1)}, f32[384]{0:T(512)}, u32[]{:S(2)}) copy-start(f32[384]{0:T(512)} %param.8) | copy-start | bytes 4612
  7.2 104.6 %copy-start.2 = (f32[384]{0:T(512)S(1)}, f32[384]{0:T(512)}, u32[]{:S(2)}) copy-start(f32[384]{0:T(512)} %param.9) | copy-start | bytes 4612
  7.2 391.6 %all-reduce.6.cloned.1.call-start = ((), (), s32[]{:S(2)}) async-start(), calls=%async_computation.1 | async-start | bytes 1990656 | tf_op jit(solution)/shard_map/psum | solution.py:53
  7.2 101.2 %collective-permute-start = (bf16[24,2,4,160]{3,2,1,0:T(4,128)(2,1)}, bf16[24,2,4,160]{3,2,1,0:T(4,128)(2,1)S(1)}, u32[]{:S(2)}, u32[]{:S(2)}) collective-permute-start(bf16[24,2,4,160]{3,2,1,0:T(4,128)(2,1)} %param.6), channel_id=1, source_target_pairs={{128,0},{256,128},{384,256},{129,1},{257,129},{385,257},{130,2},{2... | collective-permute-start | bytes 184328 | tf_op jit(solution)/shard_map/ppermute | solution.py:11
  108.6 4.9 collective-permute-start.1
  110.5 3.2 collective-permute-start.2
  128.7 545.7 %all-reduce.4.cloned.1.call-start = ((), (), s32[]{:S(2)}) async-start(), calls=%async_computation | async-start | bytes 3932160 | tf_op jit(solution)/shard_map/psum | solution.py:62
  401.7 275.6 %copy-start = (f32[24,2,4,160]{0,3,2,1:T(8,128)S(1)}, f32[24,2,4,160]{0,3,2,1:T(8,128)}, u32[]{:S(2)}) copy-start(f32[24,2,4,160]{0,3,2,1:T(8,128)} %copy.17) | copy-start | bytes 368644
Sparse Core Ops, SparseCore 0:
  128.8 269.9 all-reduce.5
  402.0 272.3 all-reduce.3
where the time goes:
time: 688 us; the launch traced here: 687 us
  waiting for transfers between devices  534 us (78%)
  blocking collectives  96.6 us (14%)
  local copies, waits for them, and re-layouts  17.4 us (3%)
  between operations  14.3 us (2%)
  other arithmetic  11.7 us (2%)
    psum x1, waiting for transfers between devices, on_device(): act_grad = lax.psum(partial_value, 'chan')  273 us
    psum x1, waiting for transfers between devices, on_device(): summed = lax.psum(local_sums, ('tm', 'height'))  262 us
    all_gather x1, blocking collectives, on_device(): whole_x = lax.all_gather(features, 'chan', axis=0, tiled=True)  96.6 us
  transfers between devices with their start and end apart: 5, of which 3 were waited for; matrix products, arithmetic and copies ran while one was open for 2% of the time, Pallas kernels for 0%

commit v1 on v0

--- a/solution.py
+++ b/solution.py
@@ -50,7 +50,7 @@
         stacked, active, (((1,), (1,)), ((), ())), preferred_element_type=jnp.float32
     )
     positions = frames * lax.axis_size("tm") * rows * lax.axis_size("height") * cols
-    summed = lax.psum(local_sums, ("tm", "height"))
+    summed = lax.psum(lax.psum(local_sums, "tm"), "height")
     weight_grad = (summed / math.sqrt(positions)).reshape(chans, 27, total)
     sig = jax.nn.sigmoid(normed)
     slope = sig * (1.0 + normed * (1.0 - sig))

time: 688 us -> 546 us (0.79)
  waiting for transfers between devices: 534 us -> 396 us
    psum x1 -> x2, waiting for transfers between devices: 262 us -> 128 us  [on_device(): summed = lax.psum(lax.psum(local_sums, 'tm'), 'height')]
  transfers between devices with their start and end apart: 5 -> 6, of which waited for: 3 -> 4; matrix products, arithmetic and copies ran while one was open for 2% -> 3% of each run, Pallas kernels for 0% -> 0%
where the time goes in v1:
time: 546 us
  waiting for transfers between devices  396 us (73%)
  blocking collectives  96.6 us (18%)
  local copies, waits for them, and re-layouts  17.4 us (3%)
  between operations  14 us (3%)
  other arithmetic  9.18 us (2%)
  matrix products  6.73 us (1%)
  starting transfers between devices  6.2 us (1%)
    psum x1, waiting for transfers between devices, on_device(): act_grad = lax.psum(partial_value, 'chan')  268 us
    psum x2, waiting for transfers between devices, on_device(): summed = lax.psum(lax.psum(local_sums, 'tm'), 'height')  128 us
    all_gather x1, blocking collectives, on_device(): whole_x = lax.all_gather(features, 'chan', axis=0, tiled=True)  96.6 us
  transfers between devices with their start and end apart: 6, of which 4 were waited for; matrix products, arithmetic and copies ran while one was open for 3% of the time, Pallas kernels for 0%

profile of v1, /device:TPU:6, one launch (start us, length us, event | category | flops | bytes accessed | tf_op | source)
XLA Modules:
  0.0 545.7 jit_solution(15198547639325217723)
XLA Ops:
  7.2 2.7 collective-permute-start
  10.0 96.6 %all_gather.3 = bf16[384,2,4,160]{3,2,1,0:T(4,128)(2,1)S(1)} all-gather(bf16[24,2,4,160]{3,2,1,0:T(4,128)(2,1)} %param.5), channel_id=1, replica_groups=mesh['tm'=4,'height'=8,'chan'=16] {'chan'}, dimensions={0}, use_global_device_ids=true | all-gather | bytes 1044480 | tf_op jit(solution)/shard_map/all_gather | solution.py:29
  106.5 1.4 copy.18
  108.0 0.4 multiply_reduce_fusion.1
  108.5 0.1 fusion.38
  108.6 1.9 collective-permute-start.1
  110.5 1.3 collective-permute-start.2
  111.8 1.7 multiply_convert_fusion
  113.5 0.2 collective-permute-done.2
  113.7 0.8 fusion.10
  114.5 0.1 fusion.37
  114.6 0.2 fusion.36
  114.9 0.2 fusion.34
  115.1 0.1 fusion.33
  115.2 0.1 fusion.32
  115.3 0.1 fusion.31
  115.5 0.2 fusion.29
  115.7 0.2 fusion.28
  115.9 0.2 fusion.26
  116.1 0.1 fusion.24
  116.2 0.1 fusion.23
  116.3 0.1 fusion.22
  116.5 0.2 fusion.20
  116.7 0.2 fusion.19
  116.9 0.1 fusion.17
  116.9 0.2 fusion.16
  117.1 0.1 fusion.15
  117.2 0.1 fusion.14
  117.4 0.1 fusion.13
  117.6 2.4 copy.19
  120.0 5.5 %reshape.64 = bf16[648,1280]{1,0:T(8,128)(2,1)S(1)} reshape(bf16[24,27,2,4,160]{4,3,2,1,0:T(4,128)(2,1)} %copy.19) | data formatting | bytes 3317760 | tf_op jit(solution)/shard_map/reshape | solution.py:48
  125.5 3.2 fusion.39
  128.7 1.1 copy.20
  129.8 1.0 reshape.65
  130.8 3.6 convolution_bitcast_fusion
  134.4 0.2 all-reduce.9.cloned.1.call-start
  134.6 0.1 rsqrt.16
  134.7 1.0 copy.17
  135.7 0.2 bitcast_convert_fusion
  136.0 51.3 %all-reduce.7.cloned.1.call-done = f32[648,384]{1,0:T(8,128)} async-done(((f32[648,384]{1,0:T(8,128)}), f32[648,384]{1,0:T(8,128)}) %all-reduce.7.cloned.1.call-update) | async-done | bytes 995344 | tf_op jit(solution)/shard_map/psum | solution.py:53
  187.3 267.5 %all-reduce.5.cloned.1.call-done = f32[384,1280]{0,1:T(8,128)} async-done(((f32[384,1280]{0,1:T(8,128)}), f32[384,1280]{0,1:T(8,128)}) %all-reduce.5.cloned.1.call-update) | async-done | bytes 1966096 | tf_op jit(solution)/shard_map/psum | solution.py:62
  454.8 3.0 multiply_reduce_fusion
  457.8 0.9 fusion.3
  458.8 0.8 copy.21
  459.6 76.6 %all-reduce.9.cloned.1.call-done = f32[648,384]{1,0:T(8,128)} async-done(((f32[648,384]{1,0:T(8,128)}), f32[648,384]{1,0:T(8,128)}) %all-reduce.9.cloned.1.call-update) | async-done | bytes 995344 | tf_op jit(solution)/shard_map/psum | solution.py:53
  536.2 1.3 broadcast_multiply_fusion
  537.5 0.1 reshape.67
  537.7 1.5 copy.22
  (27 shorter events, 0.7 us)
Async XLA Ops:
  7.2 101.2 %copy-start.1 = (bf16[24,2,4,160]{3,2,1,0:T(4,128)(2,1)S(1)}, bf16[24,2,4,160]{3,2,1,0:T(4,128)(2,1)}, u32[]{:S(2)}) copy-start(bf16[24,2,4,160]{3,2,1,0:T(4,128)(2,1)} %param.6) | copy-start | bytes 184324
  7.2 104.6 %copy-start.3 = (f32[384]{0:T(512)S(1)}, f32[384]{0:T(512)}, u32[]{:S(2)}) copy-start(f32[384]{0:T(512)} %param.8) | copy-start | bytes 4612
  7.2 104.6 %copy-start.2 = (f32[384]{0:T(512)S(1)}, f32[384]{0:T(512)}, u32[]{:S(2)}) copy-start(f32[384]{0:T(512)} %param.9) | copy-start | bytes 4612
  7.2 180.1 %all-reduce.7.cloned.1.call-start = ((), (), s32[]{:S(2)}) async-start(), calls=%async_computation.1 | async-start | bytes 1990656 | tf_op jit(solution)/shard_map/psum | solution.py:53
  7.2 101.2 %collective-permute-start = (bf16[24,2,4,160]{3,2,1,0:T(4,128)(2,1)}, bf16[24,2,4,160]{3,2,1,0:T(4,128)(2,1)S(1)}, u32[]{:S(2)}, u32[]{:S(2)}) collective-permute-start(bf16[24,2,4,160]{3,2,1,0:T(4,128)(2,1)} %param.6), channel_id=1, source_target_pairs={{128,0},{256,128},{384,256},{129,1},{257,129},{385,257},{130,2},{2... | collective-permute-start | bytes 184328 | tf_op jit(solution)/shard_map/ppermute | solution.py:11
  108.6 4.9 collective-permute-start.1
  110.5 3.2 collective-permute-start.2
  128.7 326.1 %all-reduce.5.cloned.1.call-start = ((), (), s32[]{:S(2)}) async-start(), calls=%async_computation | async-start | bytes 3932160 | tf_op jit(solution)/shard_map/psum | solution.py:62
  134.4 401.9 %all-reduce.9.cloned.1.call-start = ((), (), s32[]{:S(2)}) async-start(), calls=%async_computation.2 | async-start | bytes 1990656 | tf_op jit(solution)/shard_map/psum | solution.py:53
  454.8 3.0 copy-start
Sparse Core Ops, SparseCore 0:
  128.8 58.4 all-reduce.6
  190.5 264.2 all-reduce.4
  457.8 78.4 all-reduce.8
